TPU v7x, 32 devices: a whole 2x2x4 slice. The times are simulated.
32 devices in a mesh: dp: 4 (over y, core), seq: 8 (over z, x).
Axes of the slice: x: 2, y: 2, z: 4, core: 2. Of those that a mesh axis runs over, the one named last changes fastest.
Arguments:
- tokens: bfloat16 [2048, 6144], P('seq'), may hold values from -6 to 6
- qkv_weight: bfloat16 [6144, 3, 1024], P('seq', None, 'dp'), may hold values from -0.078125 to 0.078125
- out_weight: bfloat16 [6144, 1024], P('seq', 'dp'), may hold values from -0.25 to 0.25
- log_decay: float32 [8, 2048], P('dp', 'seq'), may hold values from -1.5 to 0, as said below
- norm_gain: float32 [1024], P('dp'), may hold values from 0.25 to 1.75
Outputs:
- mixed: bfloat16 [2048, 6144], P('seq', 'dp')
Inputs may be any that keep to these rules, and one draw needn't show every extreme that they name: `log_decay`: each entry is the logarithm of one head's decay factor at one position.
All inputs are finite; a program needn't handle non-finite values.
Results may differ from a plain program's by a relative error of at most 0.023.
Values may be sent and summed in bfloat16 or wider, within the bound.
A program may use at most 64 MiB of HBM per device.

v0:
```python
import jax
import jax.numpy as jnp
from jax import lax
from jax.sharding import PartitionSpec as P


def carried_in(value, axis, join, neutral):
    place = lax.axis_index(axis)
    gathered = jax.tree.map(
        lambda a, kind: lax.all_gather(a.astype(kind), axis), value, (jnp.bfloat16, jnp.bfloat16)
    )
    state = jax.tree.map(lambda a, e: jnp.zeros_like(a) + jnp.asarray(e, a.dtype), value, neutral)

    def one(hop, state):
        return join(
            state,
            jax.tree.map(
                lambda a, own: lax.dynamic_index_in_dim(a, hop, 0, False).astype(own.dtype),
                gathered,
                value,
            ),
        )

    return lax.fori_loop(0, place, one, state)


def combine_states(preceding_segments, later):
    return (
        preceding_segments[0] * later[0],
        later[0][:, None, None] * preceding_segments[1] + later[1],
    )


def body(tokens, qkv_weight, out_weight, log_decay, norm_gain):
    rows = tokens.shape[0]
    width = qkv_weight.shape[2]
    heads = log_decay.shape[0]
    hsize = width // heads
    proj = jnp.einsum(
        "td,dph->pth",
        tokens,
        lax.all_gather(qkv_weight, "seq", axis=0, tiled=True),
        preferred_element_type=jnp.float32,
    )
    query = jax.nn.silu(proj[0]).astype(jnp.bfloat16).reshape(rows, heads, hsize)
    lookup_vectors = jax.nn.silu(proj[1]).astype(jnp.bfloat16).reshape(rows, heads, hsize)
    value = proj[2].astype(jnp.bfloat16).reshape(rows, heads, hsize)
    cum = jnp.cumsum(log_decay, axis=1)
    scaled_key = (
        lookup_vectors.astype(jnp.float32) * jnp.exp(cum[:, -1:] - cum).T[:, :, None]
    ).astype(jnp.bfloat16)
    local = jnp.einsum("thd,the->hde", scaled_key, value, preferred_element_type=jnp.float32)
    fall = jnp.exp(cum[:, -1])
    identity = (jnp.ones((heads,), jnp.float32), jnp.zeros((heads, hsize, hsize), jnp.float32))
    prior = carried_in((fall, local), "seq", combine_states, identity)
    earlier_state = prior[1]
    later = jnp.arange(rows)[:, None] >= jnp.arange(rows)[None, :]
    scores = jnp.einsum("thd,shd->hts", query, lookup_vectors, preferred_element_type=jnp.float32)
    spread = cum[:, :, None] - cum[:, None, :]
    factor = jnp.where(later[None], jnp.exp(jnp.minimum(spread, 0.0)), 0.0)
    weights = (scores * factor).astype(jnp.bfloat16)
    intra = jnp.einsum("hts,shd->thd", weights, value, preferred_element_type=jnp.float32)
    lifted = query.astype(jnp.float32) * jnp.exp(cum).T[:, :, None]
    inter = jnp.einsum("thd,hde->the", lifted, earlier_state, precision=lax.Precision.HIGHEST)
    attn = intra + inter
    power = jnp.mean(attn * attn, axis=-1, keepdims=True)
    gain = norm_gain.reshape(heads, hsize)
    normalized_output = (
        (attn / jnp.sqrt(power + 1e-05) * gain[None]).astype(jnp.bfloat16).reshape(rows, width)
    )
    terms = jnp.einsum(
        "tg,dg->td",
        normalized_output,
        lax.all_gather(out_weight, "seq", axis=0, tiled=True),
        preferred_element_type=jnp.float32,
    )
    terms = terms.astype(jnp.bfloat16).astype(jnp.float32)
    return lax.psum_scatter(terms.astype(jnp.bfloat16), "dp", scatter_dimension=1, tiled=True)


def solution(mesh):
    in_specs = (P("seq", None), P("seq", None, "dp"), P("seq", "dp"), P("dp", "seq"), P("dp"))
    out_specs = P("seq", "dp")
    return jax.shard_map(body, mesh=mesh, in_specs=in_specs, out_specs=out_specs, check_vma=False)
```

profile of v0, /device:TPU:25, one launch (start us, length us, event | category | flops | bytes accessed | tf_op | source)
XLA Modules:
  0.0 261.8 jit_solution(7567553237243390553)
XLA Ops:
  6.5 0.0 copy-start
  6.5 0.0 all-gather.5.cloned.1.call-start
  6.5 2.6 copy.24
  9.1 0.0 all-gather.5.cloned.1.call-update
  9.1 0.0 all-gather.7.cloned.1.call-start
  9.2 0.7 all-gather.7.cloned.1.call-update
  9.9 0.0 reduce-scatter.2.cloned.1.call-start
  9.9 0.0 copy-done.3
  10.0 0.6 reduce-window.6
  10.6 0.2 slice_reduce_fusion
  10.8 0.2 reduce-window.9
  10.9 0.1 add_bitcast_fusion
  11.0 0.1 slice.30
  11.1 0.1 copy.36
  11.2 0.0 copy-done.5
  11.2 0.6 dynamic-slice
  12.4 0.2 dynamic-update-slice
  12.7 14.4 %all-reduce = bf16[16]{0:T(256)(128)(2,1)S(1)} all-reduce(bf16[16]{0:T(256)(128)(2,1)S(1)} %dynamic-update-slice), channel_id=2, replica_groups=mesh['dp'=4,'seq'=8] {'seq'}, use_global_device_ids=true, to_apply=%add | all-reduce | flops 16 | bytes 64
  27.1 0.1 reshape.96
  27.2 0.6 iota_compare_fusion
  27.8 0.1 exponential_bitcast_fusion
  27.9 118.9 %all-gather.5.cloned.1.call-done = bf16[6144,3,256]{0,2,1:T(8,128)(2,1)} async-done(((bf16[768,3,256]{0,2,1:T(8,128)(2,1)}), bf16[6144,3,256]{0,2,1:T(8,128)(2,1)}) %all-gather.5.cloned.1.call-update) | async-done | bytes 9437200 | tf_op jit(solution)/shard_map/all_gather | solution.py:42
  146.8 0.0 copy-done
  146.8 5.2 %fusion.2 = f32[3,256,256]{1,2,0:T(8,128)S(1)} fusion(bf16[6144,3,256]{0,2,1:T(8,128)(2,1)} %all-gather.5.cloned.1.call-done, bf16[256,6144]{1,0:T(8,128)(2,1)S(1)} %copy-done), kind=kOutput, calls=%fused_computation.5 | convolution fusion | flops 2415919104 | bytes 13369344 | tf_op jit(solution)/shard_map/td,dph->pth/dot_general | solution.py:39
  152.1 0.0 copy-start.2
  152.1 0.7 fusion.21
  152.8 1.8 copy.26
  154.6 0.8 copy.28
  155.4 0.0 copy-done.2
  155.4 1.3 convolution_convert_fusion.1
  156.7 0.0 copy-start.1
  156.7 27.7 %all-gather.1 = bf16[16,128,128]{2,1,0:T(8,128)(2,1)} all-gather(bf16[2,128,128]{2,1,0:T(8,128)(2,1)S(1)} %convolution_convert_fusion.1), channel_id=3, replica_groups=mesh['dp'=4,'seq'=8] {'seq'}, dimensions={0}, use_global_device_ids=true | all-gather | bytes 589824 | tf_op jit(solution)/shard_map/all_gather | solution.py:10
  184.4 2.3 fusion.6
  186.7 5.8 %while.12 = (s32[]{:T(128)}, f32[2,128,128]{2,1,0:T(8,128)S(1)}, s32[]{:T(128)}, bf16[8,2]{1,0:T(8,128)(2,1)S(1)}, bf16[8,2,128,128]{3,2,1,0:T(8,128)(2,1)}, /*index=5*/s32[]{:T(128)}, s32[]{:T(128)}, s32[]{:T(128)}) while((s32[]{:T(128)}, f32[2,128,128]{2,1,0:T(8,128)S(1)}, s32[]{:T(128)}, bf16[8,2]{1,0:T(8,128)(2,1)S(1)}, ...), condition=%wide.region_3.4_spmd, body=%wide.region_2.3_spmd.sunk | while | flops 98311 | bytes 327835 | solution.py:24
  186.7 0.9 convert_add_fusion.2
  187.7 0.9 convert_add_fusion.2
  188.6 0.9 convert_add_fusion.2
  189.6 0.9 convert_add_fusion.2
  190.6 0.9 convert_add_fusion.2
  191.5 0.9 convert_add_fusion.2
  192.5 0.0 copy-done.1
  192.5 1.5 multiply_reduce_fusion
  194.0 0.0 copy-done.4
  194.0 0.1 multiply_convert_fusion
  194.1 17.0 %all-gather.7.cloned.1.call-done = bf16[6144,256]{1,0:T(8,128)(2,1)} async-done(((bf16[768,256]{1,0:T(8,128)(2,1)}), bf16[6144,256]{1,0:T(8,128)(2,1)}) %all-gather.7.cloned.1.call-update) | async-done | bytes 3145744 | tf_op jit(solution)/shard_map/all_gather | solution.py:74
  211.1 4.6 %convolution_convert_fusion = bf16[256,6144]{1,0:T(8,128)(2,1)} fusion(bf16[256,256]{0,1:T(8,128)(2,1)S(1)} %bitcast.52, bf16[6144,256]{1,0:T(8,128)(2,1)} %all-gather.7.cloned.1.call-done), kind=kOutput, calls=%fused_computation.2 | convolution fusion | flops 806879232 | bytes 6422528 | tf_op jit(solution)/shard_map/tg,dg->td/dot_general | solution.py:71
  215.7 0.0 reduce-scatter.2.cloned.1.call-update
  215.7 39.6 %reduce-scatter.2.cloned.1.call-done = bf16[256,1536]{1,0:T(8,128)(2,1)} async-done(((bf16[256,6144]{1,0:T(8,128)(2,1)}), bf16[256,1536]{1,0:T(8,128)(2,1)}) %reduce-scatter.2.cloned.1.call-update) | async-done | bytes 786448 | tf_op jit(solution)/shard_map/reduce_scatter | solution.py:78
  (16 shorter events, 0.1 us)
Async XLA Ops:
  6.5 140.3 %copy-start = (bf16[256,6144]{1,0:T(8,128)(2,1)S(1)}, bf16[256,6144]{1,0:T(8,128)(2,1)}, u32[]{:S(2)}) copy-start(bf16[256,6144]{1,0:T(8,128)(2,1)} %param.7) | copy-start | bytes 9437188
  6.5 4.6 %copy-start.5 = (u32[32]{0:T(128)S(1)}, u32[32]{0:T(128)}, u32[]{:S(2)}) copy-start(u32[32]{0:T(128)} %constant.41) | copy-start | bytes 388
  6.5 3.4 %copy-start.3 = (f32[2,256]{1,0:T(2,128)S(1)}, f32[2,256]{1,0:T(2,128)}, u32[]{:S(2)}) copy-start(f32[2,256]{1,0:T(2,128)} %param.10) | copy-start | bytes 6148
  6.5 140.3 %all-gather.5.cloned.1.call-start = ((), (), s32[]{:S(2)}) async-start(), calls=%async_computation.1 | async-start | bytes 10616832 | tf_op jit(solution)/shard_map/all_gather | solution.py:42
  9.1 201.9 %all-gather.7.cloned.1.call-start = ((), (), s32[]{:S(2)}) async-start(), calls=%async_computation.2 | async-start | bytes 3538944 | tf_op jit(solution)/shard_map/all_gather | solution.py:74
  9.9 245.4 %reduce-scatter.2.cloned.1.call-start = ((), (), s32[]{:S(2)}) async-start(), calls=%async_computation.3 | async-start | bytes 3932160 | tf_op jit(solution)/shard_map/reduce_scatter | solution.py:78
  152.1 3.4 %copy-start.2 = (bf16[1,256,256]{1,2,0:T(8,128)(2,1)}, bf16[1,256,256]{1,2,0:T(8,128)(2,1)S(1)}, u32[]{:S(2)}) copy-start(bf16[1,256,256]{1,2,0:T(8,128)(2,1)S(1)} %slice.33) | copy-start | bytes 393220
  156.7 35.8 %copy-start.1 = (f32[256,2,128]{2,0,1:T(8,128)S(1)}, f32[256,2,128]{2,0,1:T(8,128)}, u32[]{:S(2)}) copy-start(f32[256,2,128]{2,0,1:T(8,128)} %copy.26) | copy-start | bytes 786436
  184.4 9.6 %copy-start.4 = (f32[256]{0:T(256)S(1)}, f32[256]{0:T(256)}, u32[]{:S(2)}) copy-start(f32[256]{0:T(256)} %param.11) | copy-start | bytes 3076
Sparse Core Ops, SparseCore 0:
  9.5 137.2 all-gather.4
  149.0 62.0 all-gather.6
  215.8 39.4 reduce-scatter.1
where the time goes:
time: 264 us; the launch traced here: 262 us
  waiting for transfers between devices  176 us (67%)
  blocking collectives  42 us (16%)
  matrix products  14.8 us (6%)
  between operations  13.9 us (5%)
  other arithmetic  7.34 us (3%)
  local copies, waits for them, and re-layouts  7.23 us (3%)
    all_gather x1, waiting for transfers between devices, body(): lax.all_gather(qkv_weight, 'seq', axis=0, tiled=True)  119 us
    reduce_scatter x1, waiting for transfers between devices, body(): lax.psum_scatter(terms.astype(jnp.bfloat16), 'dp', scatter_dimension=1, t...  39.6 us
    all_gather x1, blocking collectives, carried_in(): lax.all_gather(a.astype(kind), axis)  27.7 us
    all_gather x1, waiting for transfers between devices, body(): lax.all_gather(out_weight, 'seq', axis=0, tiled=True)  17 us
    unnamed x1, blocking collectives  14.4 us
    add x6, other arithmetic, combine_states(): later[0][:, None, None] * preceding_segments[1] + later[1]  5.59 us
  transfers between devices with their start and end apart: 3, of which 3 were waited for; matrix products, arithmetic and copies ran while one was open for 8% of the time, Pallas kernels for 0%

commit v1 on v0

v1 whole, which is shorter than its diff:
```python
import functools

import jax
import jax.numpy as jnp
from jax import lax
from jax.experimental import pallas as pl
from jax.experimental.pallas import tpu as pltpu
from jax.sharding import PartitionSpec as P

MESH = pl.DeviceIdType.MESH
ORDER = (1, 2, 0)


def kernel(
    nz, nd, tok, wqkv, wout, ld, gain, out,
    T, W, G, Wo, Cs, Cr, acc, N, attn, outf, sx_t, sx_r, sl_t, sl_r, dx_t, dx_r, dl_t, dl_r, state,
    loc_sem, t1_s, t1_r, t2_s, t2_r, w_s, w_r, ga_s, ga_r, gb_s, gb_r, c_s, c_r, n_s, n_r,
    sx_s, sx_rs, sl_s, sl_rs, dx_s, dx_rs, dl_s, dl_rs,
):
    d = lax.axis_index("dp")
    s = lax.axis_index("seq")
    z = s // 2
    x = s % 2
    rows = tok.shape[0]
    part = rows // nd
    wide = T.shape[2]
    half = wqkv.shape[1]
    orow, width = wout.shape
    heads, hsize = state.shape[0], state.shape[1]
    f32, bf16 = jnp.float32, jnp.bfloat16

    def dev(dd, zz, xx):
        return (dd, zz * 2 + xx)

    def up(o):
        return lax.rem(z + o, nz)

    def down(o):
        return lax.rem(z + nz - o, nz)

    def dup(o):
        return lax.rem(d + o, nd)

    def ddown(o):
        return lax.rem(d + nd - o, nd)

    def remote(src, dst, ss, rs, to):
        return pltpu.make_async_remote_copy(
            src_ref=src, dst_ref=dst, send_sem=ss, recv_sem=rs, device_id=to, device_id_type=MESH
        )

    def each(lo, hi, f):
        def step(i, carry):
            f(i)
            return carry

        lax.fori_loop(lo, hi, step, 0)

    here = dev(d, z, x)
    across = dev(d, z, 1 - x)
    mine = pl.ds(pl.multiple_of(d * part, part), part)

    barrier = pltpu.get_barrier_semaphore()
    each(1, nz, lambda o: pl.semaphore_signal(barrier, inc=1, device_id=dev(d, up(o), x), device_id_type=MESH))
    each(1, nd, lambda o: pl.semaphore_signal(barrier, inc=1, device_id=dev(dup(o), z, x), device_id_type=MESH))
    each(0, nd, lambda o: pl.semaphore_signal(barrier, inc=1, device_id=dev(dup(o), z, 1 - x), device_id_type=MESH))

    def xrows(xx, n):
        return pl.ds(pl.multiple_of(xx * n, n), n)

    cols = pl.ds(pl.multiple_of(z * wide, wide), wide)
    local_t = pltpu.make_async_copy(tok.at[:, cols], T.at[z], loc_sem.at[0])
    local_w = pltpu.make_async_copy(wqkv, W.at[:, xrows(x, half)], loc_sem.at[1])
    local_g = pltpu.make_async_copy(wout, G.at[z], loc_sem.at[2])
    local_t.start()
    local_w.start()
    local_g.start()
    pl.semaphore_wait(barrier, nz + 2 * nd - 2)

    def t1(o):
        to = pl.ds(pl.multiple_of(up(o) * wide, wide), wide)
        return remote(tok.at[mine, to], T.at[z, mine], t1_s.at[o - 1], t1_r.at[o - 1], dev(d, up(o), x))

    def t2(o, q):
        piece = T.at[down(o), mine]
        return remote(piece, piece, t2_s.at[o - 1, q - 1], t2_r.at[o - 1, q - 1], dev(dup(q), z, x))

    def wx(p):
        return remote(wqkv.at[p], W.at[p, xrows(x, half)], w_s.at[p], w_r.at[p], across)

    def ga(o):
        return remote(wout, G.at[z], ga_s.at[o - 1], ga_r.at[o - 1], dev(d, up(o), x))

    def gb(zz, xx):
        i = x if xx is x else 1 - x
        return remote(G.at[zz], Wo.at[d, xrows(x, orow)], gb_s.at[zz, i], gb_r.at[d, x], dev(zz, z, i))

    def cc(o, p):
        return remote(Cs.at[o - 1, p], Cr.at[o - 1, p], c_s.at[o - 1, p], c_r.at[o - 1, p], dev(d, up(o), x))

    def nn(q):
        return remote(N.at[d], N.at[d], n_s.at[q - 1], n_r.at[q - 1], dev(dup(q), z, x))

    def sl(o):
        return remote(sl_t, sl_r.at[o - 1], sl_s.at[o - 1], sl_rs.at[o - 1], dev(d, up(o), x))

    def dl(o):
        return remote(dl_t, dl_r.at[o - 1], dl_s.at[o - 1], dl_rs.at[o - 1], dev(d, up(o), x))

    sx = remote(sx_t, sx_r, sx_s.at[0], sx_rs.at[0], across)
    dx = remote(dx_t, dx_r, dx_s.at[0], dx_rs.at[0], across)

    each(1, nz, lambda o: t1(o).start())
    for p in ORDER:
        wx(p).start()

    it = lax.broadcasted_iota(jnp.int32, (rows, rows), 0)
    js = lax.broadcasted_iota(jnp.int32, (rows, rows), 1)
    later = it >= js
    cumc, cumr, totals = [], [], []
    for h in range(heads):
        row = ld[h : h + 1, :]
        cumc.append(jnp.sum(jnp.where(later, row, 0.0), axis=1, keepdims=True))
        column = jnp.sum(jnp.where(it == js, row, 0.0), axis=1, keepdims=True)
        cumr.append(jnp.sum(jnp.where(it <= js, column, 0.0), axis=0, keepdims=True))
        totals.append(cumc[h][rows - 1 : rows, :])
        dx_t[h : h + 1, :] = jnp.broadcast_to(totals[h], (1, dx_t.shape[1]))
    for h in range(heads, dx_t.shape[0]):
        dx_t[h : h + 1, :] = jnp.zeros((1, dx_t.shape[1]), f32)
    dx.start()

    def pass_on(o):
        t1(o).wait_recv()
        each(1, nd, lambda q: t2(o, q).start())

    each(1, nz, pass_on)
    each(1, nz, lambda o: ga(o).start())

    dx.wait_recv()
    dl_t[...] = dx_t[...] + dx_r[...]
    each(1, nz, lambda o: dl(o).start())

    local_g.wait()

    def spread(zz):
        gb(zz, None).start()

        @pl.when(zz != d)
        def _():
            gb(zz, x).start()

        @pl.when(zz == d)
        def _():
            pltpu.make_async_copy(G.at[zz], Wo.at[d, xrows(x, orow)], loc_sem.at[3]).start()

    spread(z)
    local_w.wait()
    local_t.wait()

    for p in ORDER:
        wx(p).wait_recv()

        def partial(o, p=p):
            if p == ORDER[0]:
                each(1, nd, lambda q: t2(nz - o, q).wait_recv())
            Cs[o - 1, p] = jnp.dot(T[up(o)], W[p], preferred_element_type=f32).astype(bf16)
            cc(o, p).start()

        each(1, nz, partial)
        acc[p] = jnp.dot(T[z], W[p], preferred_element_type=f32)

    def spread_later(o):
        ga(o).wait_recv()
        spread(down(o))

    each(1, nz, spread_later)

    def whole(p):
        def add(o):
            cc(o, p).wait_recv()
            acc[p] += Cr[o - 1, p].astype(f32)

        each(1, nz, add)
        return acc[p]

    def silu(u):
        return u / (1.0 + jnp.exp(-u))

    key = silu(whole(1)).astype(bf16)
    value = whole(2).astype(bf16)

    def of(a, h):
        return a[:, h * hsize : (h + 1) * hsize]

    def matmul(a, b, dims):
        return lax.dot_general(a, b, (dims, ((), ())), preferred_element_type=f32)

    own = []
    for h in range(heads):
        scaled = (of(key, h).astype(f32) * jnp.exp(totals[h] - cumc[h])).astype(bf16)
        own.append(matmul(scaled, of(value, h), ((0,), (0,))))
        sx_t[h] = own[h].astype(bf16)
    sx.start()

    query = silu(whole(0)).astype(bf16)
    for h in range(heads):
        scores = matmul(of(query, h), of(key, h), ((1,), (1,)))
        factor = jnp.where(later, jnp.exp(jnp.minimum(cumc[h] - cumr[h], 0.0)), 0.0)
        weights = (scores * factor).astype(bf16)
        attn[:, h * hsize : (h + 1) * hsize] = matmul(weights, of(value, h), ((1,), (0,)))

    sx.wait_recv()
    xf = x.astype(f32)
    for h in range(heads):
        other = sx_r[h].astype(f32)
        first = jnp.where(x == 0, own[h], other)
        second = jnp.where(x == 0, other, own[h])
        fall = jnp.exp(jnp.where(x == 0, dx_r[h : h + 1, :], dx_t[h : h + 1, :]))
        sl_t[h] = (fall * first + second).astype(bf16)

    def send_state(o):
        @pl.when(z + o < nz)
        def _():
            sl(o).start()

    each(1, nz, send_state)
    each(1, nz, lambda o: dl(o).wait_recv())
    state[...] = jnp.zeros_like(state)

    def take_state(i):
        o = nz - i

        @pl.when(z - o >= 0)
        def _():
            sl(o).wait_recv()
            for h in range(heads):
                fall = jnp.exp(dl_r[o - 1, h : h + 1, :])
                state[h] = fall * state[h] + sl_r[o - 1, h].astype(f32)

    each(1, nz, take_state)

    @pl.when(x == 1)
    def _():
        for h in range(heads):
            state[h] = jnp.exp(dx_r[h : h + 1, :]) * state[h] + sx_r[h].astype(f32)

    normed = []
    for h in range(heads):
        lifted = of(query, h).astype(f32) * jnp.exp(cumc[h])
        inter = jnp.dot(lifted, state[h], precision=lax.Precision.HIGHEST, preferred_element_type=f32)
        a = attn[:, h * hsize : (h + 1) * hsize] + inter
        power = jnp.mean(a * a, axis=1, keepdims=True)
        g = gain[:, h * hsize : (h + 1) * hsize]
        normed.append((a / jnp.sqrt(power + 1e-05) * g).astype(bf16))
    N[d] = jnp.concatenate(normed, axis=1)
    each(1, nd, lambda q: nn(q).start())

    def arrived(dd, xx):
        remote(G.at[0], Wo.at[dd, xrows(xx, orow)], gb_s.at[0, 0], gb_r.at[dd, xx], across).wait_recv()

    arrived(d, 1 - x)
    pltpu.make_async_copy(G.at[d], Wo.at[d, xrows(x, orow)], loc_sem.at[3]).wait()
    outf[...] = matmul(N[d], Wo[d], ((1,), (1,)))

    def join(q):
        dd = ddown(q)
        nn(q).wait_recv()
        arrived(dd, 0)
        arrived(dd, 1)
        outf[...] += matmul(N[dd], Wo[dd], ((1,), (1,)))

    each(1, nd, join)
    out[...] = outf[...].astype(bf16)

    def sent(o):
        t1(o).wait_send()
        ga(o).wait_send()
        dl(o).wait_send()
        each(1, nd, lambda q: t2(o, q).wait_send())
        for p in ORDER:
            cc(o, p).wait_send()

        @pl.when(z + o < nz)
        def _():
            sl(o).wait_send()

    each(1, nz, sent)
    each(1, nd, lambda q: nn(q).wait_send())
    for p in ORDER:
        wx(p).wait_send()
    sx.wait_send()
    dx.wait_send()

    def left(zz):
        gb(zz, None).wait_send()

        @pl.when(zz != d)
        def _():
            gb(zz, x).wait_send()

    each(0, nz, left)


def body(nz, nd, tokens, qkv_weight, out_weight, log_decay, norm_gain):
    rows, model = tokens.shape
    half, _, width = qkv_weight.shape
    orow = out_weight.shape[0]
    heads = log_decay.shape[0]
    hsize = width // heads
    wide = model // nz
    f32, bf16 = jnp.float32, jnp.bfloat16
    dma = pltpu.SemaphoreType.DMA
    anywhere = pl.BlockSpec(memory_space=pl.ANY)
    vmem = pl.BlockSpec(memory_space=pltpu.VMEM)
    tile = (max(8, heads), hsize)
    flops = 2 * rows * (model * 3 * width + 2 * orow * nd * width)
    return pl.pallas_call(
        functools.partial(kernel, nz, nd),
        out_shape=jax.ShapeDtypeStruct((rows, model // nd), bf16),
        in_specs=[anywhere, anywhere, anywhere, vmem, vmem],
        out_specs=vmem,
        scratch_shapes=[
            pltpu.VMEM((nz, rows, wide), bf16),
            pltpu.VMEM((3, wide, width), bf16),
            pltpu.VMEM((nz, orow, width), bf16),
            pltpu.VMEM((nd, 2 * orow, width), bf16),
            pltpu.VMEM((nz - 1, 3, rows, width), bf16),
            pltpu.VMEM((nz - 1, 3, rows, width), bf16),
            pltpu.VMEM((3, rows, width), f32),
            pltpu.VMEM((nd, rows, width), bf16),
            pltpu.VMEM((rows, width), f32),
            pltpu.VMEM((rows, 2 * orow), f32),
            pltpu.VMEM((heads, hsize, hsize), bf16),
            pltpu.VMEM((heads, hsize, hsize), bf16),
            pltpu.VMEM((heads, hsize, hsize), bf16),
            pltpu.VMEM((nz - 1, heads, hsize, hsize), bf16),
            pltpu.VMEM(tile, f32),
            pltpu.VMEM(tile, f32),
            pltpu.VMEM(tile, f32),
            pltpu.VMEM((nz - 1, *tile), f32),
            pltpu.VMEM((heads, hsize, hsize), f32),
            dma((4,)),
            dma((nz - 1,)), dma((nz - 1,)),
            dma((nz - 1, nd - 1)), dma((nz - 1, nd - 1)),
            dma((3,)), dma((3,)),
            dma((nz - 1,)), dma((nz - 1,)),
            dma((nz, 2)), dma((nd, 2)),
            dma((nz - 1, 3)), dma((nz - 1, 3)),
            dma((nd - 1,)), dma((nd - 1,)),
            dma((1,)), dma((1,)),
            dma((nz - 1,)), dma((nz - 1,)),
            dma((1,)), dma((1,)),
            dma((nz - 1,)), dma((nz - 1,)),
        ],
        compiler_params=pltpu.CompilerParams(
            collective_id=0, has_side_effects=True, vmem_limit_bytes=48 * 2**20
        ),
        cost_estimate=pl.CostEstimate(flops=flops, bytes_accessed=2 * rows * model, transcendentals=0),
    )(tokens, jnp.transpose(qkv_weight, (1, 0, 2)), out_weight, log_decay, norm_gain.reshape(1, width))


def solution(mesh):
    nd = mesh.shape["dp"]
    nz = mesh.shape["seq"] // 2
    assert nz == nd and mesh.shape["seq"] == 2 * nz
    in_specs = (P("seq", None), P("seq", None, "dp"), P("seq", "dp"), P("dp", "seq"), P("dp"))
    return jax.shard_map(
        functools.partial(body, nz, nd), mesh=mesh, in_specs=in_specs, out_specs=P("seq", "dp"), check_vma=False
    )
```

time: 264 us -> 121 us (0.46)
  waiting for transfers between devices: 176 us -> 0 us
  Pallas kernels: 0 us -> 114 us
  blocking collectives: 42 us -> 0 us
  matrix products: 14.8 us -> 0 us
  between operations: 13.9 us -> 0.01 us
  other arithmetic: 7.34 us -> 0 us
    all_gather x2 -> x0, waiting for transfers between devices: 136 us -> none  [the longest x1 119 us: body(): lax.all_gather(qkv_weight, 'seq', axis=0, tiled=True)]
    pallas_call x0 -> x1, Pallas kernels: none -> 114 us  [body(): pl.pallas_call(functools.partial(kernel, nz, nd), out_shape=jax.ShapeDtyp...]
    reduce_scatter x1 -> x0, waiting for transfers between devices: 39.6 us -> none  [body(): lax.psum_scatter(terms.astype(jnp.bfloat16), 'dp', scatter_dimension=1, t...]
    all_gather x1 -> x0, blocking collectives: 27.7 us -> none  [carried_in(): lax.all_gather(a.astype(kind), axis)]
    dot_general x5 -> x0, matrix products: 14.8 us -> none  [the longest x1 5.22 us: body(): jnp.einsum('td,dph->pth', tokens, lax.all_gather(qkv_weight, 'seq', axis=...]
    unnamed x1 -> x0, blocking collectives: 14.4 us -> none
    add x6 -> x0, other arithmetic: 5.59 us -> none  [combine_states(): later[0][:, None, None] * preceding_segments[1] + later[1]]
    unnamed x18 -> x11, local copies, waits for them, and re-layouts: 3.53 us -> 6.4 us
  transfers between devices with their start and end apart: 3 -> 0, of which waited for: 3 -> 0; matrix products, arithmetic and copies ran while one was open for 8% -> 0% of each run, Pallas kernels for 0% -> 0%
where the time goes in v1:
time: 121 us
  Pallas kernels  114 us (94%)
  local copies, waits for them, and re-layouts  6.4 us (5%)
    pallas_call x1, Pallas kernels, body(): pl.pallas_call(functools.partial(kernel, nz, nd), out_shape=jax.ShapeDtyp...  114 us
    unnamed x11, local copies, waits for them, and re-layouts  6.4 us

profile of v1, /device:TPU:25, one launch (start us, length us, event | category | flops | bytes accessed | tf_op | source)
XLA Modules:
  0.0 120.6 jit_solution(3314170162810753623)
XLA Ops:
  0.0 0.0 copy-start
  0.0 1.9 %copy-done = bf16[256,6144]{1,0:T(8,128)(2,1)S(1)} copy-done((bf16[256,6144]{1,0:T(8,128)(2,1)S(1)}, bf16[256,6144]{1,0:T(8,128)(2,1)}, u32[]{:S(2)}) %copy-start) | copy-done | bytes 3145752
  1.9 0.0 copy-start.1
  1.9 1.3 %copy-done.1 = bf16[768,3,256]{2,0,1:T(8,128)(2,1)S(1)} copy-done((bf16[768,3,256]{2,0,1:T(8,128)(2,1)S(1)}, bf16[768,3,256]{2,0,1:T(8,128)(2,1)}, u32[]{:S(2)}) %copy-start.1) | copy-done | bytes 1179672
  3.2 0.0 copy-start.2
  3.2 1.0 copy-done.2
  4.2 0.0 copy-start.3
  4.2 0.7 copy-done.3
  4.8 0.0 copy-start.4
  4.8 0.7 copy-done.4
  5.5 114.2 %shard_map.55 = bf16[256,1536]{1,0:T(8,128)(2,1)S(1)} custom-call(bf16[256,6144]{1,0:T(8,128)(2,1)S(1)} %copy-done, bf16[3,768,256]{2,1,0:T(8,128)(2,1)S(1)} %bitcast.2, bf16[768,256]{1,0:T(8,128)(2,1)S(1)} %copy-done.2, f32[2,256]{1,0:T(2,128)S(1)} %copy-done.3, f32[1,256]{1,0:T(1,128)S(1)} %bitcast.3), custom_call_target="tpu_custom_call" | custom-call | flops 3221225472 | bytes 3145728 | tf_op jit(solution)/shard_map/pallas_call | solution.py:317
  119.7 0.9 copy.7
Async XLA Ops:
  0.0 1.9 %copy-start = (bf16[256,6144]{1,0:T(8,128)(2,1)S(1)}, bf16[256,6144]{1,0:T(8,128)(2,1)}, u32[]{:S(2)}) copy-start(bf16[256,6144]{1,0:T(8,128)(2,1)} %tok.1) | copy-start | bytes 9437188
  1.9 1.3 %copy-start.1 = (bf16[768,3,256]{2,0,1:T(8,128)(2,1)S(1)}, bf16[768,3,256]{2,0,1:T(8,128)(2,1)}, u32[]{:S(2)}) copy-start(bf16[768,3,256]{2,0,1:T(8,128)(2,1)} %param.6) | copy-start | bytes 3538948
  3.2 1.0 copy-start.2
  4.2 0.7 copy-start.3
  4.8 0.7 copy-start.4

commit v2 on v1

--- a/solution.py
+++ b/solution.py
@@ -13,8 +13,8 @@
 
 def kernel(
     nz, nd, tok, wqkv, wout, ld, gain, out,
-    T, W, G, Wo, Cs, Cr, acc, N, attn, outf, sx_t, sx_r, sl_t, sl_r, dx_t, dx_r, dl_t, dl_r, state,
-    loc_sem, t1_s, t1_r, t2_s, t2_r, w_s, w_r, ga_s, ga_r, gb_s, gb_r, c_s, c_r, n_s, n_r,
+    T, W, G, Wo, Cs, Cr, P3, N, attn, outf, sx_t, sx_r, sl_t, sl_r, dx_t, dx_r, dl_t, dl_r, state,
+    loc_sem, t1_s, t1_r, t2_s, t2_r, w_s, w_r, gu_s, gu_r, gd_s, gd_r, gb_s, gb_r, c_s, c_r, n_s, n_r,
     sx_s, sx_rs, sl_s, sl_rs, dx_s, dx_rs, dl_s, dl_rs,
 ):
     d = lax.axis_index("dp")
@@ -41,8 +41,20 @@
     def dup(o):
         return lax.rem(d + o, nd)
 
-    def ddown(o):
-        return lax.rem(d + nd - o, nd)
+    def flip(v, mask):
+        bit = 1
+        while bit <= mask:
+            if mask & bit:
+                v = v + bit - 2 * bit * ((v // bit) % 2)
+            bit *= 2
+        return v
+
+    hops, held, bit = [], [0], nd // 2
+    while bit:
+        hops.append((bit, list(held)))
+        held = held + [m + bit for m in held]
+        bit //= 2
+    along = [r for r in range(1, nz) if r % 2] + [r for r in range(1, nz) if r % 2 == 0]
 
     def remote(src, dst, ss, rs, to):
         return pltpu.make_async_remote_copy(
@@ -77,29 +89,38 @@
     local_g.start()
     pl.semaphore_wait(barrier, nz + 2 * nd - 2)
 
-    def t1(o):
-        to = pl.ds(pl.multiple_of(up(o) * wide, wide), wide)
-        return remote(tok.at[mine, to], T.at[z, mine], t1_s.at[o - 1], t1_r.at[o - 1], dev(d, up(o), x))
-
-    def t2(o, q):
-        piece = T.at[down(o), mine]
-        return remote(piece, piece, t2_s.at[o - 1, q - 1], t2_r.at[o - 1, q - 1], dev(dup(q), z, x))
+    def t1(r):
+        to = pl.ds(pl.multiple_of(flip(z, r) * wide, wide), wide)
+        return remote(tok.at[mine, to], T.at[z, mine], t1_s.at[r - 1], t1_r.at[r - 1], dev(d, flip(z, r), x))
+
+    def t2(r, bit, m):
+        piece = T.at[flip(z, r), pl.ds(pl.multiple_of(flip(d, m) * part, part), part)]
+        i = m + bit - 1
+        return remote(piece, piece, t2_s.at[r - 1, i], t2_r.at[r - 1, i], dev(flip(d, bit), z, x))
 
     def wx(p):
         return remote(wqkv.at[p], W.at[p, xrows(x, half)], w_s.at[p], w_r.at[p], across)
 
-    def ga(o):
-        return remote(wout, G.at[z], ga_s.at[o - 1], ga_r.at[o - 1], dev(d, up(o), x))
+    def gup(j):
+        slot = G.at[z - j]
+        return remote(slot, slot, gu_s.at[j], gu_r.at[j], dev(d, z + 1, x))
+
+    def gdown(j):
+        slot = G.at[z + j]
+        return remote(slot, slot, gd_s.at[j], gd_r.at[j], dev(d, z - 1, x))
 
     def gb(zz, xx):
         i = x if xx is x else 1 - x
         return remote(G.at[zz], Wo.at[d, xrows(x, orow)], gb_s.at[zz, i], gb_r.at[d, x], dev(zz, z, i))
 
-    def cc(o, p):
-        return remote(Cs.at[o - 1, p], Cr.at[o - 1, p], c_s.at[o - 1, p], c_r.at[o - 1, p], dev(d, up(o), x))
-
-    def nn(q):
-        return remote(N.at[d], N.at[d], n_s.at[q - 1], n_r.at[q - 1], dev(dup(q), z, x))
+    def cc(r, p):
+        bit = r & -r
+        return remote(Cs.at[r - 1, p], Cr.at[r - 1, p], c_s.at[r - 1, p], c_r.at[r - 1, p], dev(d, flip(z, bit), x))
+
+    def nn(bit, m):
+        piece = N.at[flip(d, m)]
+        i = m + bit - 1
+        return remote(piece, piece, n_s.at[i], n_r.at[i], dev(flip(d, bit), z, x))
 
     def sl(o):
         return remote(sl_t, sl_r.at[o - 1], sl_s.at[o - 1], sl_rs.at[o - 1], dev(d, up(o), x))
@@ -110,7 +131,8 @@
     sx = remote(sx_t, sx_r, sx_s.at[0], sx_rs.at[0], across)
     dx = remote(dx_t, dx_r, dx_s.at[0], dx_rs.at[0], across)
 
-    each(1, nz, lambda o: t1(o).start())
+    for r in along:
+        t1(r).start()
     for p in ORDER:
         wx(p).start()
 
@@ -129,19 +151,26 @@
         dx_t[h : h + 1, :] = jnp.zeros((1, dx_t.shape[1]), f32)
     dx.start()
 
-    def pass_on(o):
-        t1(o).wait_recv()
-        each(1, nd, lambda q: t2(o, q).start())
-
-    each(1, nz, pass_on)
-    each(1, nz, lambda o: ga(o).start())
+    for r in along:
+        t1(r).wait_recv()
+        t2(r, hops[0][0], 0).start()
+
+    def hop(j):
+        @pl.when((z - j >= 0) & (z + 1 < nz))
+        def _():
+            gup(j).start()
+
+        @pl.when((z + j < nz) & (z - 1 >= 0))
+        def _():
+            gdown(j).start()
+
+    local_g.wait()
+    hop(0)
 
     dx.wait_recv()
     dl_t[...] = dx_t[...] + dx_r[...]
     each(1, nz, lambda o: dl(o).start())
 
-    local_g.wait()
-
     def spread(zz):
         gb(zz, None).start()
 
@@ -154,34 +183,72 @@
             pltpu.make_async_copy(G.at[zz], Wo.at[d, xrows(x, orow)], loc_sem.at[3]).start()
 
     spread(z)
+    def came(j):
+        @pl.when(z - 1 - j >= 0)
+        def _():
+            remote(G.at[z - 1 - j], G.at[z - 1 - j], gu_s.at[j], gu_r.at[j], here).wait_recv()
+
+        @pl.when(z + 1 + j < nz)
+        def _():
+            remote(G.at[z + 1 + j], G.at[z + 1 + j], gd_s.at[j], gd_r.at[j], here).wait_recv()
+
+        if j + 1 < nz - 1:
+            hop(j + 1)
+
+        @pl.when(z - 1 - j >= 0)
+        def _():
+            spread(z - 1 - j)
+
+        @pl.when(z + 1 + j < nz)
+        def _():
+            spread(z + 1 + j)
+
     local_w.wait()
     local_t.wait()
 
+    for k in range(1, len(hops)):
+        before, sent_before = hops[k - 1]
+        for r in along:
+            for m in sent_before:
+                t2(r, before, m).wait_recv()
+            for m in hops[k][1]:
+                t2(r, hops[k][0], m).start()
+    last, sent_last = hops[-1]
     for p in ORDER:
         wx(p).wait_recv()
-
-        def partial(o, p=p):
-            if p == ORDER[0]:
-                each(1, nd, lambda q: t2(nz - o, q).wait_recv())
-            Cs[o - 1, p] = jnp.dot(T[up(o)], W[p], preferred_element_type=f32).astype(bf16)
-            cc(o, p).start()
-
-        each(1, nz, partial)
-        acc[p] = jnp.dot(T[z], W[p], preferred_element_type=f32)
-
-    def spread_later(o):
-        ga(o).wait_recv()
-        spread(down(o))
-
-    each(1, nz, spread_later)
+        for r in along + [0]:
+            if p == ORDER[0] and r:
+                for m in sent_last:
+                    t2(r, last, m).wait_recv()
+            product = jnp.dot(T[flip(z, r)], W[p], preferred_element_type=f32)
+            if r % 2:
+                Cs[r - 1, p] = product.astype(bf16)
+                cc(r, p).start()
+            else:
+                P3[r // 2, p] = product
+        if p == ORDER[0]:
+            came(0)
+
+    for j in range(1, nz - 2):
+        came(j)
+    bit = 2
+    while bit < nz:
+        for p in ORDER:
+            for r in list(range(bit, nz, 2 * bit)) + list(range(0, nz, 2 * bit)):
+                cc(r + bit // 2, p).wait_recv()
+                total = P3[r // 2, p] + Cr[r + bit // 2 - 1, p].astype(f32)
+                if r % (2 * bit):
+                    Cs[r - 1, p] = total.astype(bf16)
+                    cc(r, p).start()
+                else:
+                    P3[r // 2, p] = total
+        bit *= 2
+    if nz > 2:
+        came(nz - 2)
 
     def whole(p):
-        def add(o):
-            cc(o, p).wait_recv()
-            acc[p] += Cr[o - 1, p].astype(f32)
-
-        each(1, nz, add)
-        return acc[p]
+        cc(nz // 2, p).wait_recv()
+        return P3[0, p] + Cr[nz // 2 - 1, p].astype(f32)
 
     def silu(u):
         return u / (1.0 + jnp.exp(-u))
@@ -253,7 +320,7 @@
         g = gain[:, h * hsize : (h + 1) * hsize]
         normed.append((a / jnp.sqrt(power + 1e-05) * g).astype(bf16))
     N[d] = jnp.concatenate(normed, axis=1)
-    each(1, nd, lambda q: nn(q).start())
+    nn(hops[0][0], 0).start()
 
     def arrived(dd, xx):
         remote(G.at[0], Wo.at[dd, xrows(xx, orow)], gb_s.at[0, 0], gb_r.at[dd, xx], across).wait_recv()
@@ -262,30 +329,48 @@
     pltpu.make_async_copy(G.at[d], Wo.at[d, xrows(x, orow)], loc_sem.at[3]).wait()
     outf[...] = matmul(N[d], Wo[d], ((1,), (1,)))
 
-    def join(q):
-        dd = ddown(q)
-        nn(q).wait_recv()
-        arrived(dd, 0)
-        arrived(dd, 1)
-        outf[...] += matmul(N[dd], Wo[dd], ((1,), (1,)))
-
-    each(1, nd, join)
+    for k, (bit, pieces) in enumerate(hops):
+        for m in pieces:
+            nn(bit, m).wait_recv()
+        if k + 1 < len(hops):
+            for m in hops[k + 1][1]:
+                nn(hops[k + 1][0], m).start()
+        for m in pieces:
+            dd = flip(d, m + bit)
+            arrived(dd, 0)
+            arrived(dd, 1)
+            outf[...] += matmul(N[dd], Wo[dd], ((1,), (1,)))
+
     out[...] = outf[...].astype(bf16)
 
     def sent(o):
-        t1(o).wait_send()
-        ga(o).wait_send()
         dl(o).wait_send()
-        each(1, nd, lambda q: t2(o, q).wait_send())
+
+        @pl.when(z + o < nz)
+        def _():
+            sl(o).wait_send()
+
+    each(1, nz, sent)
+    for r in along:
+        t1(r).wait_send()
+        for bit, pieces in hops:
+            for m in pieces:
+                t2(r, bit, m).wait_send()
         for p in ORDER:
-            cc(o, p).wait_send()
-
-        @pl.when(z + o < nz)
-        def _():
-            sl(o).wait_send()
-
-    each(1, nz, sent)
-    each(1, nd, lambda q: nn(q).wait_send())
+            cc(r, p).wait_send()
+    for bit, pieces in hops:
+        for m in pieces:
+            nn(bit, m).wait_send()
+    for j in range(nz - 1):
+
+        @pl.when((z - j >= 0) & (z + 1 < nz))
+        def _(j=j):
+            gup(j).wait_send()
+
+        @pl.when((z + j < nz) & (z - 1 >= 0))
+        def _(j=j):
+            gdown(j).wait_send()
+
     for p in ORDER:
         wx(p).wait_send()
     sx.wait_send()
@@ -326,7 +411,7 @@
             pltpu.VMEM((nd, 2 * orow, width), bf16),
             pltpu.VMEM((nz - 1, 3, rows, width), bf16),
             pltpu.VMEM((nz - 1, 3, rows, width), bf16),
-            pltpu.VMEM((3, rows, width), f32),
+            pltpu.VMEM((nz // 2, 3, rows, width), f32),
             pltpu.VMEM((nd, rows, width), bf16),
             pltpu.VMEM((rows, width), f32),
             pltpu.VMEM((rows, 2 * orow), f32),
@@ -344,6 +429,7 @@
             dma((nz - 1, nd - 1)), dma((nz - 1, nd - 1)),
             dma((3,)), dma((3,)),
             dma((nz - 1,)), dma((nz - 1,)),
+            dma((nz - 1,)), dma((nz - 1,)),
             dma((nz, 2)), dma((nd, 2)),
             dma((nz - 1, 3)), dma((nz - 1, 3)),
             dma((nd - 1,)), dma((nd - 1,)),
@@ -353,7 +439,7 @@
             dma((nz - 1,)), dma((nz - 1,)),
         ],
         compiler_params=pltpu.CompilerParams(
-            collective_id=0, has_side_effects=True, vmem_limit_bytes=48 * 2**20
+            collective_id=0, has_side_effects=True, vmem_limit_bytes=61 * 2**20
         ),
         cost_estimate=pl.CostEstimate(flops=flops, bytes_accessed=2 * rows * model, transcendentals=0),
     )(tokens, jnp.transpose(qkv_weight, (1, 0, 2)), out_weight, log_decay, norm_gain.reshape(1, width))
@@ -362,7 +448,7 @@
 def solution(mesh):
     nd = mesh.shape["dp"]
     nz = mesh.shape["seq"] // 2
-    assert nz == nd and mesh.shape["seq"] == 2 * nz
+    assert nz == nd and nz & (nz - 1) == 0 and nz > 1 and mesh.shape["seq"] == 2 * nz
     in_specs = (P("seq", None), P("seq", None, "dp"), P("seq", "dp"), P("dp", "seq"), P("dp"))
     return jax.shard_map(
         functools.partial(body, nz, nd), mesh=mesh, in_specs=in_specs, out_specs=P("seq", "dp"), check_vma=False

time: 121 us -> 105 us (0.87)
  Pallas kernels: 114 us -> 103 us
  local copies, waits for them, and re-layouts: 6.4 us -> 2.06 us
    pallas_call x1, Pallas kernels: 114 us -> 103 us  [body(): pl.pallas_call(functools.partial(kernel, nz, nd), out_shape=jax.ShapeDtyp...]
    unnamed x11 -> x1, local copies, waits for them, and re-layouts: 6.4 us -> 2.06 us
where the time goes in v2:
time: 105 us
  Pallas kernels  103 us (98%)
  local copies, waits for them, and re-layouts  2.06 us (2%)
    pallas_call x1, Pallas kernels, body(): pl.pallas_call(functools.partial(kernel, nz, nd), out_shape=jax.ShapeDtyp...  103 us

profile of v2, /device:TPU:25, one launch (start us, length us, event | category | flops | bytes accessed | tf_op | source)
XLA Modules:
  0.0 105.0 jit_solution(17832172799310123384)
XLA Ops:
  0.0 102.9 %shard_map.55 = bf16[256,1536]{1,0:T(8,128)(2,1)} custom-call(bf16[256,6144]{1,0:T(8,128)(2,1)} %tok.1, bf16[3,768,256]{2,1,0:T(8,128)(2,1)} %bitcast.2, bf16[768,256]{1,0:T(8,128)(2,1)} %wout.1, f32[2,256]{1,0:T(2,128)} %ld.1, f32[1,256]{1,0:T(1,128)} %bitcast.3), custom_call_target="tpu_custom_call" | custom-call | flops 3221225472 | bytes 3145728 | tf_op jit(solution)/shard_map/pallas_call | solution.py:402
  102.9 2.1 %copy.7 = bf16[256,1536]{1,0:T(8,128)(2,1)} copy(bf16[256,1536]{1,0:T(8,128)(2,1)} %shard_map.55) | data formatting | bytes 1572864

commit v3 on v2

--- a/solution.py
+++ b/solution.py
@@ -131,10 +131,22 @@
     sx = remote(sx_t, sx_r, sx_s.at[0], sx_rs.at[0], across)
     dx = remote(dx_t, dx_r, dx_s.at[0], dx_rs.at[0], across)
 
+    def hop(j):
+        @pl.when((z - j >= 0) & (z + 1 < nz))
+        def _():
+            gup(j).start()
+
+        @pl.when((z + j < nz) & (z - 1 >= 0))
+        def _():
+            gdown(j).start()
+
+
     for r in along:
         t1(r).start()
     for p in ORDER:
         wx(p).start()
+    local_g.wait()
+    hop(0)
 
     it = lax.broadcasted_iota(jnp.int32, (rows, rows), 0)
     js = lax.broadcasted_iota(jnp.int32, (rows, rows), 1)
@@ -155,17 +167,6 @@
         t1(r).wait_recv()
         t2(r, hops[0][0], 0).start()
 
-    def hop(j):
-        @pl.when((z - j >= 0) & (z + 1 < nz))
-        def _():
-            gup(j).start()
-
-        @pl.when((z + j < nz) & (z - 1 >= 0))
-        def _():
-            gdown(j).start()
-
-    local_g.wait()
-    hop(0)
 
     dx.wait_recv()
     dl_t[...] = dx_t[...] + dx_r[...]
@@ -214,6 +215,7 @@
             for m in hops[k][1]:
                 t2(r, hops[k][0], m).start()
     last, sent_last = hops[-1]
+    came(0)
     for p in ORDER:
         wx(p).wait_recv()
         for r in along + [0]:
@@ -226,10 +228,10 @@
                 cc(r, p).start()
             else:
                 P3[r // 2, p] = product
-        if p == ORDER[0]:
-            came(0)
-
-    for j in range(1, nz - 2):
+        if p == ORDER[0] and nz > 2:
+            came(1)
+
+    for j in range(2, nz - 1):
         came(j)
     bit = 2
     while bit < nz:
@@ -243,8 +245,6 @@
                 else:
                     P3[r // 2, p] = total
         bit *= 2
-    if nz > 2:
-        came(nz - 2)
 
     def whole(p):
         cc(nz // 2, p).wait_recv()

time: 105 us -> 95.5 us (0.910)
  Pallas kernels: 103 us -> 93.3 us
    pallas_call x1, Pallas kernels: 103 us -> 93.3 us  [body(): pl.pallas_call(functools.partial(kernel, nz, nd), out_shape=jax.ShapeDtyp...]
where the time goes in v3:
time: 95.5 us; the launch traced here: 95.3 us
  Pallas kernels  93.3 us (98%)
  local copies, waits for them, and re-layouts  2.06 us (2%)
    pallas_call x1, Pallas kernels, body(): pl.pallas_call(functools.partial(kernel, nz, nd), out_shape=jax.ShapeDtyp...  93.3 us
    unnamed x1, local copies, waits for them, and re-layouts  2.06 us

profile of v3, /device:TPU:25, one launch (start us, length us, event | category | flops | bytes accessed | tf_op | source)
XLA Modules:
  0.0 95.3 jit_solution(11383578167872468241)
XLA Ops:
  0.0 93.3 %shard_map.55 = bf16[256,1536]{1,0:T(8,128)(2,1)} custom-call(bf16[256,6144]{1,0:T(8,128)(2,1)} %tok.1, bf16[3,768,256]{2,1,0:T(8,128)(2,1)} %bitcast.2, bf16[768,256]{1,0:T(8,128)(2,1)} %wout.1, f32[2,256]{1,0:T(2,128)} %ld.1, f32[1,256]{1,0:T(1,128)} %bitcast.3), custom_call_target="tpu_custom_call" | custom-call | flops 3221225472 | bytes 3145728 | tf_op jit(solution)/shard_map/pallas_call | solution.py:402
  93.3 2.1 %copy.7 = bf16[256,1536]{1,0:T(8,128)(2,1)} copy(bf16[256,1536]{1,0:T(8,128)(2,1)} %shard_map.55) | data formatting | bytes 1572864
